TPU v7x, 512 devices: a whole 4x8x8 slice. The times are simulated.
512 devices in a mesh: freq: 16 (over z, y_hi), strip: 32 (over x, y_lo, core).
Axes of the slice: x: 4, y: 8 (y_hi: 2, y_lo: 4; y = y_hi * 4 + y_lo), z: 8, core: 2. Of those that a mesh axis runs over, the one named last changes fastest.
Arguments:
- receiver_field: float32 [2, 16, 256, 2048], P(None, 'freq', 'strip'), may hold values from -17 to 17
- source_field: float32 [2, 16, 256, 2048], P(None, 'freq', 'strip'), may hold values from -4 to 4
- velocity_class: int32 [256, 2048], P('strip'), may hold values from 0 to 7
- filters: float32 [16, 8, 2, 9], P('freq'), may hold values from -0.8 to 0.8
- point_spread: float32 [16, 2, 15, 15], replicated, may hold values from -0.05 to 1
- spread_index: int32 [32, 16], replicated, may hold values from 0 to 15
Outputs:
- migrated: float32 [256, 2, 2048], P('strip', None, 'freq')
- reflectivity: float32 [256, 2, 2048], P('strip', None, 'freq')
- misfit: float32 [], replicated
All inputs are finite; a program needn't handle non-finite values.
Results may differ from a plain program's by a relative error of at most 0.0003.
Values sent between devices are 32-bit elements; how exact they have to be, the bound alone decides.
No kernel may reach another device: no remote copies, remote signals or barrier semaphores. Data moves between devices by JAX's collectives and lax.ppermute only.
A program may use at most 64 MiB of HBM per device.

v0:
```python
import math
import jax
import jax.numpy as jnp
from jax import lax
from jax.sharding import PartitionSpec as P

STEPS = 2
NCLASS = 8
PASSES = 2
HIGHEST = lax.Precision.HIGHEST


def extended_2(cells, sides, width):
    for axis, dim in sides:
        count = lax.axis_size(axis)
        ends = count - 1
        head = lax.slice_in_dim(cells, 0, width, axis=dim)
        tail = lax.slice_in_dim(cells, cells.shape[dim] - width, cells.shape[dim], axis=dim)
        cells = jnp.concatenate(
            [
                lax.ppermute(tail, axis, [(i, (i + 1) % count) for i in range(ends)]),
                cells,
                lax.ppermute(head, axis, [((i + 1) % count, i) for i in range(ends)]),
            ],
            axis=dim,
        )
    return cells


def class_maps(classes, filters):
    levels = jnp.arange(NCLASS, dtype=jnp.int32)
    chosen = jnp.where(classes[None] == levels[:, None, None], 1.0, 0.0)
    planes = jnp.einsum("fcpt,cxy->ptfxy", filters, chosen, precision=HIGHEST)
    taps_real = [planes[0, tap_index] for tap_index in range(9)]
    taps_imag = [planes[1, tap_index] for tap_index in range(9)]
    return (taps_real, taps_imag)


def advance(wavefield, taps_real, taps_imag, factor):
    row_count = wavefield.shape[2] - 2
    col_count = wavefield.shape[3]
    padded = jnp.pad(wavefield, ((0, 0), (0, 0), (0, 0), (1, 1)))
    real_part = jnp.zeros(taps_real[0].shape, jnp.float32)
    imag_part = jnp.zeros(taps_real[0].shape, jnp.float32)
    for tap_index in range(9):
        row_shift = tap_index // 3
        col_shift = tap_index % 3
        near_real = padded[
            0, :, row_shift : row_shift + row_count, col_shift : col_shift + col_count
        ]
        near_imag = padded[
            1, :, row_shift : row_shift + row_count, col_shift : col_shift + col_count
        ]
        coef_real = taps_real[tap_index]
        coef_imag = factor * taps_imag[tap_index]
        real_part = real_part + coef_real * near_real - coef_imag * near_imag
        imag_part = imag_part + coef_real * near_imag + coef_imag * near_real
    return jnp.stack([real_part, imag_part])


def correlate(receiver, source):
    return jnp.sum(receiver[0] * source[0] + receiver[1] * source[1], axis=0)


def lag_pick(lag_count):
    depths = jnp.arange(lag_count, dtype=jnp.int32)
    spacing = jnp.abs(depths[:, None] - depths[None, :])
    return jnp.where(spacing[None] == depths[:, None, None], 1.0, 0.0)


def convolve(extended, toeplitz, out_rows, picker):
    shifted = jnp.stack(
        [extended[shift_row : shift_row + out_rows] for shift_row in range(toeplitz.shape[0])],
        axis=2,
    )
    mixed = jnp.einsum("xdas,asly->xdly", shifted, toeplitz, precision=HIGHEST)
    return jnp.einsum("xdly,lde->xey", mixed, picker, precision=HIGHEST)


def local(receiver_field, source_field, velocity_class, filters, point_spread, spread_index):
    per_device = receiver_field.shape[1]
    row_count = receiver_field.shape[2]
    strips = lax.axis_size("strip")
    groups = lax.axis_size("freq")
    scaling = 1.0 / math.sqrt(per_device * groups)
    image_terms = []
    taps_real, taps_imag = class_maps(velocity_class, filters)
    receiver = receiver_field
    source = source_field
    for depth_step in range(STEPS):
        wide_receiver, wide_source = (
            extended_2(receiver, (("strip", 2),), 1),
            extended_2(source, (("strip", 2),), 1),
        )
        receiver = advance(wide_receiver, taps_real, taps_imag, 1.0)
        source = advance(wide_source, taps_real, taps_imag, -1.0)
        image_terms.append(correlate(receiver, source))
    partial_value = jnp.stack(image_terms, axis=1)
    whole = lax.psum(partial_value, "freq")
    share = whole.shape[2] // groups
    migrated = lax.dynamic_slice_in_dim(whole, lax.axis_index("freq") * share, share, 2)
    migrated = migrated * scaling
    col_count = migrated.shape[2]
    kernel_side = point_spread.shape[2]
    reach = kernel_side // 2
    wide_cols = col_count + 2 * reach
    picker = lag_pick(point_spread.shape[1])
    brick_row = lax.axis_index("strip")
    brick_col = lax.axis_index("freq")

    def brick_kernel(row_step, col_step):
        row_at = jnp.clip(brick_row + row_step, 0, strips - 1)
        col_at = jnp.clip(brick_col + col_step, 0, groups - 1)
        chosen = lax.dynamic_index_in_dim(
            lax.dynamic_index_in_dim(spread_index, row_at, 0, False), col_at, 0, False
        )
        return lax.dynamic_index_in_dim(point_spread, chosen, 0, False)

    columns = jnp.arange(wide_cols, dtype=jnp.int32)[:, None]
    outputs = jnp.arange(col_count, dtype=jnp.int32)[None, :]
    offsets = jnp.arange(kernel_side, dtype=jnp.int32)[:, None, None]
    band_forward = jnp.where(columns[None] - outputs[None] == offsets, 1.0, 0.0)
    band_adjoint = jnp.where(outputs[None] + 2 * reach - columns[None] == offsets, 1.0, 0.0)
    table_forward = jnp.einsum("lab,bsy->asly", brick_kernel(0, 0), band_forward, precision=HIGHEST)
    region = jnp.where(columns[:, 0] < reach, 0, jnp.where(columns[:, 0] < reach + col_count, 1, 2))
    region_pick = jnp.where(region[:, None] == jnp.arange(3, dtype=jnp.int32)[None, :], 1.0, 0.0)

    def table_adjoint(row_step):
        flipped = jnp.stack(
            [jnp.flip(brick_kernel(row_step, col_step), axis=1) for col_step in (-1, 0, 1)]
        )
        per_column = jnp.einsum("sj,jlab->slab", region_pick, flipped, precision=HIGHEST)
        return jnp.einsum("slab,bsw->aslw", per_column, band_adjoint, precision=HIGHEST)

    table_upper = table_adjoint(-1)
    table_middle = table_adjoint(0)
    table_lower = table_adjoint(1)

    def extend_rim(values):
        return extended_2(values, (("freq", 2), ("strip", 0)), reach)

    def measure(residual):
        return lax.psum(jnp.sum(residual * residual), ("freq", "strip"))

    cell_count = float(migrated.shape[1] * row_count * strips * col_count * groups)
    residual = -migrated
    reflectivity = jnp.zeros_like(migrated)
    energy = measure(residual)
    for pass_index in range(PASSES):
        weight = 1.0 / jnp.sqrt(residual * residual + energy / cell_count)
        extended = extend_rim(weight * residual)
        positions = jnp.arange(row_count + 2 * reach, dtype=jnp.int32)[:, None, None]
        middle = extended * jnp.where(
            (positions >= reach) & (positions < reach + row_count), 1.0, 0.0
        )
        summed = convolve(middle, table_middle, row_count, picker)
        upper = extended[: 3 * reach] * jnp.where(positions[: 3 * reach] < reach, 1.0, 0.0)
        lower = extended[row_count - reach :] * jnp.where(
            positions[row_count - reach :] >= row_count + reach, 1.0, 0.0
        )
        summed = summed.at[:reach].add(convolve(upper, table_upper, reach, picker))
        summed = summed.at[row_count - reach :].add(convolve(lower, table_lower, reach, picker))
        image_of = convolve(extend_rim(summed), table_forward, row_count, picker)
        grad_square, curvature = lax.psum(
            (jnp.sum(summed * summed), jnp.sum(weight * image_of * image_of)), ("freq", "strip")
        )
        step_length = grad_square / curvature
        reflectivity = reflectivity - step_length * summed
        residual = residual - step_length * image_of
        energy = measure(residual)
    return (migrated, reflectivity, energy / cell_count)


def solution(mesh):
    return jax.shard_map(
        local,
        mesh=mesh,
        in_specs=(
            P(None, "freq", "strip", None),
            P(None, "freq", "strip", None),
            P("strip", None),
            P("freq", None, None, None),
            P(),
            P(),
        ),
        out_specs=(P("strip", None, "freq"), P("strip", None, "freq"), P()),
        check_vma=False,
    )
```

profile of v0, /device:TPU:1, one launch (start us, length us, event | category | flops | bytes accessed | tf_op | source)
XLA Modules:
  0.0 950.9 jit_solution(10511014915909429593)
XLA Ops:
  8.9 4.6 collective-permute-start.2
  13.5 6.1 collective-permute-start.3
  23.1 3.0 collective-permute-start.1
  45.8 3.2 constant_dynamic-slice_fusion.2
  57.8 3.9 copy.109
  61.7 3.7 convolution_bitcast_fusion.2
  65.4 3.7 convolution_bitcast_fusion.3
  73.1 3.9 copy.102
  89.1 4.1 fusion.282
  97.8 3.6 collective-permute-start.4
  103.8 2.7 collective-permute-done.5
  106.9 4.6 fusion.281
  112.3 5.4 convolution_bitcast_fusion.4
  117.8 193.8 %all-reduce.8.cloned.1.call-done = f32[8,2,2048]{2,1,0:T(2,128)} async-done(((f32[8,2,2048]{2,1,0:T(2,128)}), f32[8,2,2048]{2,1,0:T(2,128)}) %all-reduce.8.cloned.1.call-update) | async-done | bytes 131088 | tf_op jit(solution)/shard_map/psum | solution.py:99
  312.9 106.4 %psum.57 = f32[]{:T(128)} all-reduce(f32[]{:T(128)} %get-tuple-element.61), channel_id=1, replica_groups=mesh['freq'=16,'strip'=32] {'freq','strip'}, use_global_device_ids=true, to_apply=%region_2.3 | all-reduce | flops 1 | bytes 8 | tf_op jit(solution)/shard_map/psum | solution.py:143
  420.0 5.6 collective-permute-start.8
  427.0 7.0 collective-permute-done.9
  436.7 2.8 collective-permute-start.11
  442.5 4.2 fusion.14
  452.8 6.0 collective-permute-start.12
  462.1 5.0 collective-permute-done.13
  467.2 3.4 collective-permute-start.14
  479.3 103.4 %all-reduce.5 = (f32[]{:T(128)}, f32[]{:T(128)}) all-reduce(f32[]{:T(128)} %multiply_reduce_fusion.2, f32[]{:T(128)} %get-tuple-element.117), channel_id=1, replica_groups=mesh['freq'=16,'strip'=32] {'freq','strip'}, use_global_device_ids=true, to_apply=%region_4.5 | all-reduce | flops 2 | bytes 16 | tf_op jit(solution)/shard_map/psum | solution.py:164
  584.6 95.3 %psum.60 = f32[]{:T(128)} all-reduce(f32[]{:T(128)} %get-tuple-element.57), channel_id=1, replica_groups=mesh['freq'=16,'strip'=32] {'freq','strip'}, use_global_device_ids=true, to_apply=%region_8.9 | all-reduce | flops 1 | bytes 8 | tf_op jit(solution)/shard_map/psum | solution.py:143
  680.6 4.8 collective-permute-start.16
  686.8 7.0 collective-permute-done.17
  701.9 4.1 fusion.4
  712.4 6.5 collective-permute-start.20
  720.3 7.0 collective-permute-done.21
  727.4 3.4 collective-permute-start.22
  739.5 104.5 %all-reduce.4 = (f32[]{:T(128)}, f32[]{:T(128)}) all-reduce(f32[]{:T(128)} %multiply_reduce_fusion.1, f32[]{:T(128)} %get-tuple-element.119), channel_id=1, replica_groups=mesh['freq'=16,'strip'=32] {'freq','strip'}, use_global_device_ids=true, to_apply=%region_10.11 | all-reduce | flops 2 | bytes 16 | tf_op jit(solution)/shard_map/psum | solution.py:164
  846.6 95.3 %psum.63 = f32[]{:T(128)} all-reduce(f32[]{:T(128)} %multiply_reduce_fusion), channel_id=1, replica_groups=mesh['freq'=16,'strip'=32] {'freq','strip'}, use_global_device_ids=true, to_apply=%region_14.15 | all-reduce | flops 1 | bytes 8 | tf_op jit(solution)/shard_map/psum | solution.py:143
  (282 shorter events, 94.6 us)
Async XLA Ops:
  7.2 38.7 %copy-start.4 = (f32[16,2,15,15]{0,1,3,2:T(2,128)S(1)}, f32[16,2,15,15]{0,1,3,2:T(2,128)}, u32[]{:S(2)}) copy-start(f32[16,2,15,15]{0,1,3,2:T(2,128)} %param.18) | copy-start | bytes 86404
  7.2 304.4 %all-reduce.8.cloned.1.call-start = ((), (), s32[]{:S(2)}) async-start(), calls=%async_computation | async-start | bytes 262144 | tf_op jit(solution)/shard_map/psum | solution.py:99
  8.9 68.2 %collective-permute-start.2 = (f32[2,1,1,2048]{3,0,2,1:T(2,128)}, f32[2,1,1,2048]{3,0,2,1:T(2,128)}, u32[]{:S(2)}, u32[]{:S(2)}) collective-permute-start(f32[2,1,1,2048]{3,0,2,1:T(2,128)} %get-tuple-element.82), channel_id=1, source_target_pairs={{0,1},{1,2},{2,3},{3,4},{4,5},{5,6},{6,7},{7,8},{8,9},{9,10},{10,1... | collective-permute-start | bytes 49160 | tf_op jit(solution)/shard_map/ppermute | solution.py:21
  13.5 64.4 %collective-permute-start.3 = (f32[2,1,1,2048]{3,0,2,1:T(2,128)}, f32[2,1,1,2048]{3,0,2,1:T(2,128)}, u32[]{:S(2)}, u32[]{:S(2)}) collective-permute-start(f32[2,1,1,2048]{3,0,2,1:T(2,128)} %get-tuple-element.83), channel_id=1, source_target_pairs={{1,0},{2,1},{3,2},{4,3},{5,4},{6,5},{7,6},{8,7},{9,8},{10,9},{11,1... | collective-permute-start | bytes 49160 | tf_op jit(solution)/shard_map/ppermute | solution.py:23
  21.2 62.0 %collective-permute-start = (f32[2,1,1,2048]{3,0,2,1:T(2,128)}, f32[2,1,1,2048]{3,0,2,1:T(2,128)}, u32[]{:S(2)}, u32[]{:S(2)}) collective-permute-start(f32[2,1,1,2048]{3,0,2,1:T(2,128)} %get-tuple-element.78), channel_id=1, source_target_pairs={{0,1},{1,2},{2,3},{3,4},{4,5},{5,6},{6,7},{7,8},{8,9},{9,10},{10,1... | collective-permute-start | bytes 49160 | tf_op jit(solution)/shard_map/ppermute | solution.py:21
  23.1 61.0 %collective-permute-start.1 = (f32[2,1,1,2048]{3,0,2,1:T(2,128)}, f32[2,1,1,2048]{3,0,2,1:T(2,128)}, u32[]{:S(2)}, u32[]{:S(2)}) collective-permute-start(f32[2,1,1,2048]{3,0,2,1:T(2,128)} %get-tuple-element.79), channel_id=1, source_target_pairs={{1,0},{2,1},{3,2},{4,3},{5,4},{6,5},{7,6},{8,7},{9,8},{10,9},{11,1... | collective-permute-start | bytes 49160 | tf_op jit(solution)/shard_map/ppermute | solution.py:23
  71.2 6.6 copy-start.8
  93.2 10.1 %collective-permute-start.6 = (f32[2,1,1,2048]{3,0,2,1:T(2,128)S(1)}, f32[2,1,1,2048]{3,0,2,1:T(2,128)S(1)}, u32[]{:S(2)}, u32[]{:S(2)}) collective-permute-start(f32[2,1,1,2048]{3,0,2,1:T(2,128)S(1)} %get-tuple-element.73), channel_id=1, source_target_pairs={{0,1},{1,2},{2,3},{3,4},{4,5},{5,6},{6,7},{7,8},{8,9},{9,10},{10,1... | collective-permute-start | bytes 49160 | tf_op jit(solution)/shard_map/ppermute | solution.py:21
  95.8 7.6 collective-permute-start.7
  97.8 6.0 collective-permute-start.4
  101.4 5.1 collective-permute-start.5
  112.3 329.5 %copy-start.13 = (f32[21]{0:T(128)S(1)}, f32[21]{0:T(128)}, u32[]{:S(2)}) copy-start(f32[21]{0:T(128)} %fusion.337) | copy-start | bytes 256
  117.8 329.3 %copy-start.2 = (f32[15,142,2,128,1]{3,0,2,1,4:T(8,128)S(1)}, f32[15,142,2,128,1]{3,0,2,1,4:T(8,128)}, u32[]{:S(2)}) copy-start(f32[15,142,2,128,1]{3,0,2,1,4:T(8,128)} %convolution_bitcast_fusion.2) | copy-start | bytes 6543364
  312.9 271.1 %copy-start.10 = (f32[8,2,128]{2,1,0:T(2,128)}, f32[8,2,128]{2,1,0:T(2,128)S(1)}, u32[]{:S(2)}) copy-start(f32[8,2,128]{2,1,0:T(2,128)S(1)} %get-tuple-element.62) | copy-start | bytes 24580
  420.0 7.0 collective-permute-start.8
  425.6 8.3 collective-permute-start.9
  434.0 5.5 collective-permute-start.10
  436.7 5.0 collective-permute-start.11
  442.5 7.0 copy-start
  452.8 9.3 collective-permute-start.12
  458.7 8.3 collective-permute-start.13
  467.2 6.1 collective-permute-start.14
  470.5 5.0 collective-permute-start.15
  680.5 25.7 %copy-start.1 = (f32[15,142,2,128,1]{3,0,2,1,4:T(8,128)S(1)}, f32[15,142,2,128,1]{3,0,2,1,4:T(8,128)}, u32[]{:S(2)}) copy-start(f32[15,142,2,128,1]{3,0,2,1,4:T(8,128)} %convolution_bitcast_fusion.3) | copy-start | bytes 6543364
  680.6 6.1 collective-permute-start.16
  685.4 8.3 collective-permute-start.17
  693.9 5.3 collective-permute-start.18
  696.5 5.0 collective-permute-start.19
  712.4 7.8 collective-permute-start.20
  719.0 8.3 collective-permute-start.21
  727.4 5.9 collective-permute-start.22
  730.8 5.0 collective-permute-start.23
  (8 other events, 34.6 us)
Sparse Core Ops, SparseCore 0:
  112.4 199.0 all-reduce.7
where the time goes:
time: 962 us; the launch traced here: 951 us
  blocking collectives  505 us (52%)
  waiting for transfers between devices  232 us (24%)
  starting transfers between devices  75.2 us (8%)
  matrix products  45.8 us (5%)
  between operations  38.4 us (4%)
  local copies, waits for them, and re-layouts  28.9 us (3%)
  other arithmetic  26 us (3%)
    psum x3, blocking collectives, measure(): return lax.psum(jnp.sum(residual * residual), ('freq', 'strip'))  297 us
    psum x2, blocking collectives, local(): lax.psum((jnp.sum(summed * summed), jnp.sum(weight * image_of * image_of)...  208 us
    psum x1, waiting for transfers between devices, local(): whole = lax.psum(partial_value, 'freq')  194 us
    ppermute x12, starting transfers between devices, extended_2(): lax.ppermute(tail, axis, [(i, (i + 1) % count) for i in range(ends)])  47.6 us
    ppermute x12, waiting for transfers between devices, extended_2(): lax.ppermute(head, axis, [((i + 1) % count, i) for i in range(ends)])  37.9 us
    ppermute x12, starting transfers between devices, extended_2(): lax.ppermute(head, axis, [((i + 1) % count, i) for i in range(ends)])  27.6 us
    dot_general x8, matrix products, convolve(): mixed = jnp.einsum('xdas,asly->xdly', shifted, toeplitz, precision=HIGHEST)  23 us
  transfers between devices with their start and end apart: 25, of which 10 were waited for; matrix products, arithmetic and copies ran while one was open for 5% of the time, Pallas kernels for 0%

commit v1 on v0

--- a/solution.py
+++ b/solution.py
@@ -162,7 +162,8 @@
         summed = summed.at[row_count - reach :].add(convolve(lower, table_lower, reach, picker))
         image_of = convolve(extend_rim(summed), table_forward, row_count, picker)
         grad_square, curvature = lax.psum(
-            (jnp.sum(summed * summed), jnp.sum(weight * image_of * image_of)), ("freq", "strip")
+            lax.psum((jnp.sum(summed * summed), jnp.sum(weight * image_of * image_of)), "strip"),
+            "freq",
         )
         step_length = grad_square / curvature
         reflectivity = reflectivity - step_length * summed

time: 962 us -> 990 us (1.029)
  blocking collectives: 505 us -> 532 us
    psum x0 -> x2, blocking collectives: none -> 85.9 us  [local(): lax.psum(lax.psum((jnp.sum(summed * summed), jnp.sum(weight * image_of *...]
    psum x2, blocking collectives: 208 us -> 131 us  [local(): lax.psum((jnp.sum(summed * summed), jnp.sum(weight * image_of * image_of)...]
    psum x3, blocking collectives: 297 us -> 315 us  [measure(): return lax.psum(jnp.sum(residual * residual), ('freq', 'strip'))]
where the time goes in v1:
time: 990 us; the launch traced here: 979 us
  blocking collectives  532 us (54%)
  waiting for transfers between devices  233 us (24%)
  starting transfers between devices  75.4 us (8%)
  matrix products  45.8 us (5%)
  between operations  38.8 us (4%)
  local copies, waits for them, and re-layouts  28.9 us (3%)
  other arithmetic  25.9 us (3%)
    psum x3, blocking collectives, measure(): return lax.psum(jnp.sum(residual * residual), ('freq', 'strip'))  315 us
    psum x1, waiting for transfers between devices, local(): whole = lax.psum(partial_value, 'freq')  194 us
    psum x2, blocking collectives, local(): lax.psum((jnp.sum(summed * summed), jnp.sum(weight * image_of * image_of)...  131 us
    psum x2, blocking collectives, local(): lax.psum(lax.psum((jnp.sum(summed * summed), jnp.sum(weight * image_of *...  85.9 us
    ppermute x12, starting transfers between devices, extended_2(): lax.ppermute(tail, axis, [(i, (i + 1) % count) for i in range(ends)])  48.5 us
    ppermute x12, waiting for transfers between devices, extended_2(): lax.ppermute(head, axis, [((i + 1) % count, i) for i in range(ends)])  38.9 us
    ppermute x12, starting transfers between devices, extended_2(): lax.ppermute(head, axis, [((i + 1) % count, i) for i in range(ends)])  26.9 us
    dot_general x8, matrix products, convolve(): mixed = jnp.einsum('xdas,asly->xdly', shifted, toeplitz, precision=HIGHEST)  23 us
  transfers between devices with their start and end apart: 25, of which 10 were waited for; matrix products, arithmetic and copies ran while one was open for 5% of the time, Pallas kernels for 0%

profile of v1, /device:TPU:1, one launch (start us, length us, event | category | flops | bytes accessed | tf_op | source)
XLA Modules:
  0.0 979.2 jit_solution(12839582832089551212)
XLA Ops:
  8.9 4.6 collective-permute-start.2
  13.5 6.1 collective-permute-start.3
  46.2 3.2 constant_dynamic-slice_fusion.2
  58.1 3.9 copy.109
  62.0 3.7 convolution_bitcast_fusion.2
  65.7 3.7 convolution_bitcast_fusion.3
  73.4 3.9 copy.102
  89.3 4.1 fusion.282
  98.1 3.6 collective-permute-start.4
  107.2 4.6 fusion.281
  112.6 5.4 convolution_bitcast_fusion.4
  118.0 193.8 %all-reduce.10.cloned.1.call-done = f32[8,2,2048]{2,1,0:T(2,128)} async-done(((f32[8,2,2048]{2,1,0:T(2,128)}), f32[8,2,2048]{2,1,0:T(2,128)}) %all-reduce.10.cloned.1.call-update) | async-done | bytes 131088 | tf_op jit(solution)/shard_map/psum | solution.py:99
  313.1 106.4 %psum.85 = f32[]{:T(128)} all-reduce(f32[]{:T(128)} %get-tuple-element.65), channel_id=1, replica_groups=mesh['freq'=16,'strip'=32] {'freq','strip'}, use_global_device_ids=true, to_apply=%region_2.3 | all-reduce | flops 1 | bytes 8 | tf_op jit(solution)/shard_map/psum | solution.py:143
  420.2 5.6 collective-permute-start.8
  427.2 7.0 collective-permute-done.9
  442.8 4.2 fusion.14
  453.0 6.0 collective-permute-start.12
  462.3 5.0 collective-permute-done.13
  467.4 3.4 collective-permute-start.14
  479.5 65.4 %all-reduce.5 = (f32[]{:T(128)}, f32[]{:T(128)}) all-reduce(f32[]{:T(128)} %multiply_reduce_fusion.2, f32[]{:T(128)} %get-tuple-element.121), channel_id=1, replica_groups=mesh['freq'=16,'strip'=32] {'strip'}, use_global_device_ids=true, to_apply=%region_4.5 | all-reduce | flops 2 | bytes 16 | tf_op jit(solution)/shard_map/psum | solution.py:165
  544.9 43.5 %all-reduce.7 = (f32[]{:T(128)}, f32[]{:T(128)}) all-reduce(f32[]{:T(128)} %get-tuple-element.53, f32[]{:T(128)} %get-tuple-element.54), channel_id=1, replica_groups=mesh['freq'=16,'strip'=32] {'freq'}, use_global_device_ids=true, to_apply=%region_5.6 | all-reduce | flops 2 | bytes 16 | tf_op jit(solution)/shard_map/psum | solution.py:164
  590.4 103.0 %psum.90 = f32[]{:T(128)} all-reduce(f32[]{:T(128)} %get-tuple-element.61), channel_id=1, replica_groups=mesh['freq'=16,'strip'=32] {'freq','strip'}, use_global_device_ids=true, to_apply=%region_10.11 | all-reduce | flops 1 | bytes 8 | tf_op jit(solution)/shard_map/psum | solution.py:143
  694.2 4.0 collective-permute-start.16
  699.5 7.3 collective-permute-done.17
  706.9 5.3 collective-permute-start.18
  717.7 4.1 fusion.4
  728.2 5.6 collective-permute-start.20
  735.1 7.0 collective-permute-done.21
  742.2 3.4 collective-permute-start.22
  754.3 65.4 %all-reduce.4 = (f32[]{:T(128)}, f32[]{:T(128)}) all-reduce(f32[]{:T(128)} %multiply_reduce_fusion.1, f32[]{:T(128)} %get-tuple-element.123), channel_id=1, replica_groups=mesh['freq'=16,'strip'=32] {'strip'}, use_global_device_ids=true, to_apply=%region_12.13 | all-reduce | flops 2 | bytes 16 | tf_op jit(solution)/shard_map/psum | solution.py:165
  819.7 42.3 %all-reduce.6 = (f32[]{:T(128)}, f32[]{:T(128)}) all-reduce(f32[]{:T(128)} %get-tuple-element.51, f32[]{:T(128)} %get-tuple-element.52), channel_id=1, replica_groups=mesh['freq'=16,'strip'=32] {'freq'}, use_global_device_ids=true, to_apply=%region_13.14 | all-reduce | flops 2 | bytes 16 | tf_op jit(solution)/shard_map/psum | solution.py:164
  864.6 105.6 %psum.95 = f32[]{:T(128)} all-reduce(f32[]{:T(128)} %multiply_reduce_fusion), channel_id=1, replica_groups=mesh['freq'=16,'strip'=32] {'freq','strip'}, use_global_device_ids=true, to_apply=%region_18.19 | all-reduce | flops 1 | bytes 8 | tf_op jit(solution)/shard_map/psum | solution.py:143
  (284 shorter events, 100.5 us)
Async XLA Ops:
  7.2 39.0 %copy-start.4 = (f32[16,2,15,15]{0,1,3,2:T(2,128)S(1)}, f32[16,2,15,15]{0,1,3,2:T(2,128)}, u32[]{:S(2)}) copy-start(f32[16,2,15,15]{0,1,3,2:T(2,128)} %param.18) | copy-start | bytes 86404
  7.2 304.6 %all-reduce.10.cloned.1.call-start = ((), (), s32[]{:S(2)}) async-start(), calls=%async_computation | async-start | bytes 262144 | tf_op jit(solution)/shard_map/psum | solution.py:99
  8.9 68.4 %collective-permute-start.2 = (f32[2,1,1,2048]{3,0,2,1:T(2,128)}, f32[2,1,1,2048]{3,0,2,1:T(2,128)}, u32[]{:S(2)}, u32[]{:S(2)}) collective-permute-start(f32[2,1,1,2048]{3,0,2,1:T(2,128)} %get-tuple-element.86), channel_id=1, source_target_pairs={{0,1},{1,2},{2,3},{3,4},{4,5},{5,6},{6,7},{7,8},{8,9},{9,10},{10,1... | collective-permute-start | bytes 49160 | tf_op jit(solution)/shard_map/ppermute | solution.py:21
  13.5 64.7 %collective-permute-start.3 = (f32[2,1,1,2048]{3,0,2,1:T(2,128)}, f32[2,1,1,2048]{3,0,2,1:T(2,128)}, u32[]{:S(2)}, u32[]{:S(2)}) collective-permute-start(f32[2,1,1,2048]{3,0,2,1:T(2,128)} %get-tuple-element.87), channel_id=1, source_target_pairs={{1,0},{2,1},{3,2},{4,3},{5,4},{6,5},{7,6},{8,7},{9,8},{10,9},{11,1... | collective-permute-start | bytes 49160 | tf_op jit(solution)/shard_map/ppermute | solution.py:23
  21.2 62.3 %collective-permute-start = (f32[2,1,1,2048]{3,0,2,1:T(2,128)}, f32[2,1,1,2048]{3,0,2,1:T(2,128)}, u32[]{:S(2)}, u32[]{:S(2)}) collective-permute-start(f32[2,1,1,2048]{3,0,2,1:T(2,128)} %get-tuple-element.82), channel_id=1, source_target_pairs={{0,1},{1,2},{2,3},{3,4},{4,5},{5,6},{6,7},{7,8},{8,9},{9,10},{10,1... | collective-permute-start | bytes 49160 | tf_op jit(solution)/shard_map/ppermute | solution.py:21
  23.1 61.3 %collective-permute-start.1 = (f32[2,1,1,2048]{3,0,2,1:T(2,128)}, f32[2,1,1,2048]{3,0,2,1:T(2,128)}, u32[]{:S(2)}, u32[]{:S(2)}) collective-permute-start(f32[2,1,1,2048]{3,0,2,1:T(2,128)} %get-tuple-element.83), channel_id=1, source_target_pairs={{1,0},{2,1},{3,2},{4,3},{5,4},{6,5},{7,6},{8,7},{9,8},{10,9},{11,1... | collective-permute-start | bytes 49160 | tf_op jit(solution)/shard_map/ppermute | solution.py:23
  71.5 6.6 copy-start.8
  93.5 10.1 %collective-permute-start.6 = (f32[2,1,1,2048]{3,0,2,1:T(2,128)S(1)}, f32[2,1,1,2048]{3,0,2,1:T(2,128)S(1)}, u32[]{:S(2)}, u32[]{:S(2)}) collective-permute-start(f32[2,1,1,2048]{3,0,2,1:T(2,128)S(1)} %get-tuple-element.77), channel_id=1, source_target_pairs={{0,1},{1,2},{2,3},{3,4},{4,5},{5,6},{6,7},{7,8},{8,9},{9,10},{10,1... | collective-permute-start | bytes 49160 | tf_op jit(solution)/shard_map/ppermute | solution.py:21
  96.1 7.6 collective-permute-start.7
  98.1 6.0 collective-permute-start.4
  101.7 5.1 collective-permute-start.5
  112.6 329.5 %copy-start.13 = (f32[21]{0:T(128)S(1)}, f32[21]{0:T(128)}, u32[]{:S(2)}) copy-start(f32[21]{0:T(128)} %fusion.337) | copy-start | bytes 256
  118.0 329.3 %copy-start.2 = (f32[15,142,2,128,1]{3,0,2,1,4:T(8,128)S(1)}, f32[15,142,2,128,1]{3,0,2,1,4:T(8,128)}, u32[]{:S(2)}) copy-start(f32[15,142,2,128,1]{3,0,2,1,4:T(8,128)} %convolution_bitcast_fusion.2) | copy-start | bytes 6543364
  313.1 276.7 %copy-start.10 = (f32[8,2,128]{2,1,0:T(2,128)}, f32[8,2,128]{2,1,0:T(2,128)S(1)}, u32[]{:S(2)}) copy-start(f32[8,2,128]{2,1,0:T(2,128)S(1)} %get-tuple-element.66) | copy-start | bytes 24580
  420.2 7.0 collective-permute-start.8
  425.9 8.3 collective-permute-start.9
  434.3 5.5 collective-permute-start.10
  436.9 5.0 collective-permute-start.11
  442.8 7.0 copy-start
  453.0 9.3 collective-permute-start.12
  459.0 8.3 collective-permute-start.13
  467.4 6.1 collective-permute-start.14
  470.8 5.0 collective-permute-start.15
  694.1 27.9 %copy-start.1 = (f32[15,142,2,128,1]{3,0,2,1,4:T(8,128)S(1)}, f32[15,142,2,128,1]{3,0,2,1,4:T(8,128)}, u32[]{:S(2)}) copy-start(f32[15,142,2,128,1]{3,0,2,1,4:T(8,128)} %convolution_bitcast_fusion.3) | copy-start | bytes 6543364
  694.2 5.3 collective-permute-start.16
  698.2 8.6 collective-permute-start.17
  706.9 7.2 collective-permute-start.18
  712.2 5.0 collective-permute-start.19
  728.2 6.9 collective-permute-start.20
  733.7 8.3 collective-permute-start.21
  742.2 5.9 collective-permute-start.22
  745.5 5.0 collective-permute-start.23
  (8 other events, 34.5 us)
Sparse Core Ops, SparseCore 0:
  112.7 199.0 all-reduce.9
